TPU v7x, 32 devices: a whole 2x2x4 slice. The times are simulated.
32 devices in a mesh: leaf: 4 (over z), row: 2 (over core), col: 4 (over y, x).
Axes of the slice: x: 2, y: 2, z: 4, core: 2. Of those that a mesh axis runs over, the one named last changes fastest.
Arguments:
- leaf_rhs: float32 [4, 2048, 256], P('leaf'), may hold values from -6 to 6
- root_rhs: float32 [8, 128, 256], P(None, None, ('row', 'col')), may hold values from -6 to 6
- leaf_inverse: float32 [4, 2048, 2048], P('leaf', ('row', 'col')), as said below
- coupling: float32 [4, 8, 128, 2048], P('leaf', None, None, ('row', 'col')), may hold values from -0.0625 to 0.0625
- coupled: int32 [4, 8], P('leaf'), may hold values 0 or 1
- root_inverse: float32 [8, 128, 128], replicated
- root_lower: float32 [8, 8, 128, 128], replicated, may hold values from -0.09375 to 0.09375
Outputs:
- leaf_solution: float32 [4, 2048, 256], P('leaf', ('row', 'col'))
- root_solution: float32 [8, 128, 256], P(None, None, ('row', 'col'))
Inputs may be any that keep to these rules, and one draw needn't show every extreme that they name: leaf_inverse[i] and root_inverse[k] are lower triangular with positive diagonals.
All inputs are finite; a program needn't handle non-finite values. No bound on the sum of `coupled` on one device may be relied on, other than what follows from the above.
Results may differ from a plain program's by a relative error of at most 0.0001.
Values sent between devices are 32-bit elements; how exact they have to be, the bound alone decides.
A program may use at most 64 MiB of HBM per device.

v0:
```python
import jax
import jax.numpy as jnp
from jax import lax
from jax.sharding import PartitionSpec as P


def per_device(leaf_rhs, root_rhs, leaf_inverse, coupling, coupled, root_inverse, root_lower):
    high = lax.Precision.HIGHEST
    rhs = leaf_rhs[0]
    inverse_rows = leaf_inverse[0]
    blocks = coupling[0]
    pattern = coupled[0].astype(jnp.float32)
    supernodes = root_rhs.shape[0]
    narrow = root_rhs.shape[2]
    solved = jnp.dot(inverse_rows, rhs, precision=high)
    term = jnp.einsum("kwn,nq->kwq", blocks, solved, precision=high) * pattern[:, None, None]
    total = lax.psum(term, ("leaf", "row", "col"))
    offset = lax.axis_index(("row", "col")) * narrow
    summed = lax.dynamic_slice_in_dim(total, offset, narrow, 2)
    pending = root_rhs - summed
    forward_parts = []
    for step in range(supernodes):
        others = pending[step]
        for earlier in range(step):
            others = others - jnp.dot(
                root_lower[step, earlier], forward_parts[earlier], precision=high
            )
        forward_parts.append(jnp.dot(root_inverse[step], others, precision=high))
    back_parts = [None] * supernodes
    for step in range(supernodes - 1, -1, -1):
        others = forward_parts[step]
        for later in range(step + 1, supernodes):
            others = others - jnp.dot(root_lower[later, step].T, back_parts[later], precision=high)
        back_parts[step] = jnp.dot(root_inverse[step].T, others, precision=high)
    root_mine = jnp.stack(back_parts, 0)
    full_root = lax.all_gather(root_mine, ("row", "col"), axis=2, tiled=True)
    weighted = full_root * pattern[:, None, None]
    residual = solved - jnp.einsum("kwn,kwq->nq", blocks, weighted, precision=high)
    leaf_part = lax.psum_scatter(
        lax.dot_general(inverse_rows, residual, (((0,), (0,)), ((), ())), precision=high),
        ("row", "col"),
        scatter_dimension=0,
        tiled=True,
    )
    return (leaf_part[None], root_mine)


def solution(mesh):
    in_specs = (
        P("leaf", None, None),
        P(None, None, ("row", "col")),
        P("leaf", ("row", "col"), None),
        P("leaf", None, None, ("row", "col")),
        P("leaf", None),
        P(),
        P(),
    )
    out_specs = (P("leaf", ("row", "col"), None), P(None, None, ("row", "col")))
    return jax.shard_map(
        per_device, mesh=mesh, in_specs=in_specs, out_specs=out_specs, check_vma=False
    )
```

profile of v0, /device:TPU:0, one launch (start us, length us, event | category | flops | bytes accessed | tf_op | source)
XLA Modules:
  0.0 295.7 jit_solution(10974754133899853628)
XLA Ops:
  8.8 3.5 %fusion = f32[256,256]{1,0:T(8,128)S(1)} fusion(f32[1,2048,256]{2,1,0:T(8,128)} %param.7, f32[1,256,2048]{2,1,0:T(8,128)S(1)} %copy-done), kind=kOutput, calls=%fused_computation.1 | convolution fusion | flops 1610612736 | bytes 4456448 | tf_op jit(solution)/shard_map/dot_general | solution.py:15
  12.3 2.9 fusion.4
  15.3 132.7 %all-reduce.2.cloned.1.call-done = f32[8,128,256]{1,2,0:T(8,128)} async-done(((f32[8,128,256]{1,2,0:T(8,128)}), f32[8,128,256]{1,2,0:T(8,128)}) %all-reduce.2.cloned.1.call-update) | async-done | bytes 1048592 | tf_op jit(solution)/shard_map/psum | solution.py:17
  148.9 1.0 fusion.125
  150.0 1.1 fusion.13
  151.1 1.0 fusion.19
  152.1 1.0 fusion.24
  153.2 1.0 fusion.28
  154.3 1.0 fusion.31
  155.3 1.0 fusion.33
  156.4 1.0 fusion.34
  157.5 1.0 fusion.120
  158.5 1.1 fusion.12
  159.6 1.0 fusion.18
  160.6 1.0 fusion.23
  161.7 1.0 fusion.27
  162.8 1.0 fusion.30
  163.8 1.0 fusion.32
  164.9 1.0 fusion.112
  165.9 1.1 fusion.11
  167.0 1.0 fusion.17
  168.1 1.0 fusion.22
  169.2 1.0 fusion.26
  170.2 1.0 fusion.29
  171.3 1.0 fusion.102
  172.3 1.1 fusion.10
  173.4 1.0 fusion.16
  174.5 1.0 fusion.21
  175.5 1.0 fusion.25
  176.6 1.0 fusion.90
  177.6 1.1 fusion.9
  178.7 1.0 fusion.15
  179.8 1.0 fusion.20
  180.9 1.0 fusion.76
  181.9 1.1 fusion.8
  183.0 1.0 fusion.14
  184.1 1.0 fusion.60
  185.1 1.1 fusion.7
  186.6 1.0 convolution_subtract_fusion.27
  187.8 1.0 convolution_subtract_fusion.26
  190.0 1.0 convolution_subtract_fusion.24
  193.2 1.0 convolution_subtract_fusion.21
  197.4 1.0 convolution_subtract_fusion.17
  217.2 22.4 %all-gather.2.cloned.1.call-done = f32[8,128,256]{1,2,0:T(8,128)} async-done(((f32[8,128,32]{1,2,0:T(8,128)}), f32[8,128,256]{1,2,0:T(8,128)}) %all-gather.2.cloned.1.call-update) | async-done | bytes 1048592 | tf_op jit(solution)/shard_map/all_gather | solution.py:36
  239.6 3.1 %fusion.5 = f32[256,256]{1,0:T(8,128)S(1)} fusion(f32[256,256]{1,0:T(8,128)S(1)} %fusion, f32[1,8,128,256]{3,2,1,0:T(8,128)S(1)} %copy-done.1, f32[8,128,256]{1,2,0:T(8,128)} %all-gather.2.cloned.1.call-done, f32[8]{0:T(128)S(1)} %convert_bitcast_fusion), kind=kOutput, calls=%fused_computation.8 | convolution fusion | flops 805634048 | bytes 2621472 | tf_op jit(solution)/shard_map/kwn,kwq->nq/dot_general | solution.py:38
  242.7 3.3 %convolution_bitcast_fusion = f32[2048,256]{0,1:T(8,128)} fusion(f32[256,256]{1,0:T(8,128)S(1)} %fusion.5, f32[1,256,2048]{2,1,0:T(8,128)S(1)} %copy-done), kind=kOutput, calls=%fused_computation | convolution fusion | flops 1610612736 | bytes 4456448 | tf_op jit(solution)/shard_map/dot_general | solution.py:40
  246.0 41.4 %reduce-scatter.2.cloned.1.call-done = f32[256,256]{0,1:T(8,128)} async-done(((f32[2048,256]{0,1:T(8,128)}), f32[256,256]{0,1:T(8,128)}) %reduce-scatter.2.cloned.1.call-update) | async-done | bytes 262160 | tf_op jit(solution)/shard_map/reduce_scatter | solution.py:39
  287.3 1.8 copy.10
  (57 shorter events, 28.1 us)
Async XLA Ops:
  7.2 1.6 copy-start
  7.2 5.1 %copy-start.1 = (f32[1,8,128,256]{3,2,1,0:T(8,128)S(1)}, f32[1,8,128,256]{3,2,1,0:T(8,128)}, u32[]{:S(2)}) copy-start(f32[1,8,128,256]{3,2,1,0:T(8,128)} %param.10) | copy-start | bytes 3145732
  7.2 140.8 %copy-start.4 = (f32[8,128,32]{1,2,0:T(8,128)S(1)}, f32[8,128,32]{1,2,0:T(8,128)}, u32[]{:S(2)}) copy-start(f32[8,128,32]{1,2,0:T(8,128)} %param.8) | copy-start | bytes 393220
  7.2 140.8 %all-reduce.2.cloned.1.call-start = ((), (), s32[]{:S(2)}) async-start(), calls=%async_computation.1 | async-start | bytes 2097152 | tf_op jit(solution)/shard_map/psum | solution.py:17
  15.2 224.4 %all-gather.2.cloned.1.call-start = ((), (), s32[]{:S(2)}) async-start(), calls=%async_computation.2 | async-start | bytes 1179648 | tf_op jit(solution)/shard_map/all_gather | solution.py:36
  148.0 38.2 %copy-start.2 = (f32[8,128,128]{2,1,0:T(8,128)S(1)}, f32[8,128,128]{2,1,0:T(8,128)}, u32[]{:S(2)}) copy-start(f32[8,128,128]{2,1,0:T(8,128)} %param.12) | copy-start | bytes 1572868
  216.3 0.7 copy-start.3
  217.0 70.4 %reduce-scatter.2.cloned.1.call-start = ((), (), s32[]{:S(2)}) async-start(), calls=%async_computation.3 | async-start | bytes 2359296 | tf_op jit(solution)/shard_map/reduce_scatter | solution.py:39
Sparse Core Ops, SparseCore 0:
  15.4 132.5 all-reduce.1
  217.1 22.4 all-gather.1
  246.1 41.2 reduce-scatter.1
where the time goes:
time: 299 us; the launch traced here: 296 us
  waiting for transfers between devices  196 us (66%)
  matrix products  78.6 us (26%)
  between operations  15.2 us (5%)
  local copies, waits for them, and re-layouts  3.21 us (1%)
    psum x1, waiting for transfers between devices, per_device(): total = lax.psum(term, ('leaf', 'row', 'col'))  133 us
    reduce_scatter x1, waiting for transfers between devices, per_device(): lax.psum_scatter(lax.dot_general(inverse_rows, residual, (((0,), (0,)), (...  41.4 us
    dot_general x28, matrix products, per_device(): jnp.dot(root_lower[step, earlier], forward_parts[earlier], precision=high)  29.1 us
    dot_general x28, matrix products, per_device(): jnp.dot(root_lower[later, step].T, back_parts[later], precision=high)  28.1 us
    all_gather x1, waiting for transfers between devices, per_device(): full_root = lax.all_gather(root_mine, ('row', 'col'), axis=2, tiled=True)  22.4 us
    dot_general x8, matrix products, per_device(): forward_parts.append(jnp.dot(root_inverse[step], others, precision=high))  7.41 us
  transfers between devices with their start and end apart: 3, of which 3 were waited for; matrix products, arithmetic and copies ran while one was open for 0% of the time, Pallas kernels for 0%

commit v1 on v0

v1 whole, which is shorter than its diff:
```python
import functools

import jax
import jax.numpy as jnp
from jax import lax
from jax.experimental import pallas as pl
from jax.experimental.pallas import tpu as pltpu
from jax.sharding import PartitionSpec as P

F32 = jnp.float32
BF16 = jnp.bfloat16
MESH = pl.DeviceIdType.MESH
NN = (((1,), (0,)), ((), ()))
NT = (((1,), (1,)), ((), ()))


def split(value):
    high = value.astype(BF16)
    return high, (value - high.astype(F32)).astype(BF16)


def mul(a, b, dims=NN):
    dot = functools.partial(lax.dot_general, dimension_numbers=dims, preferred_element_type=F32)
    return dot(a[0], b[0]) + (dot(a[0], b[1]) + dot(a[1], b[0]))


def kernel(
    sizes,
    rhs_hbm, root_rhs_hbm, inverse_hbm, coupling_hbm, coupled_ref, root_inverse_hbm, root_lower_hbm,
    leaf_out, root_out,
    rhs_v, inverse_v, coupling_v, root_rhs_v, root_inverse_v, root_lower_v,
    solved, turned, turned_hi, turned_lo, coup_hi, coup_lo, inv_hi, inv_lo,
    t_full, t_hi, t_lo,
    term, pair_in, pair_sum, cols_in, slab, slab_in, mine, gathered,
    root_all, resid_hi, resid_lo, part, part_in, part_cols,
    load_sem, rhs_sem, inv_sem,
    pair_sem, cols_sem, leaf_sem, back_sem, root_sem, root_pair_sem, fin_pair_sem, fin_sem,
):
    leaves, cols, seps, width, order, rows, nrhs = sizes
    narrow = nrhs // (2 * cols)
    groups = narrow // 8
    per = groups * seps // leaves
    step = rows
    chunks = order // step
    l = lax.axis_index("leaf")
    r = lax.axis_index("row")
    c = lax.axis_index("col")

    def turn(value, by, count):
        return lax.rem(value + by, count)

    def at_row(x):
        return {"leaf": l, "row": x, "col": c}

    def at_col(x):
        return {"leaf": l, "row": r, "col": x}

    def at_leaf(x):
        return {"leaf": x, "row": r, "col": c}

    def remote(src, dst, sem, i, where):
        return pltpu.make_async_remote_copy(
            src_ref=src, dst_ref=dst, send_sem=sem.at[0, i], recv_sem=sem.at[1, i],
            device_id=where, device_id_type=MESH,
        )

    def inv_load(m):
        return pltpu.make_async_copy(
            inverse_hbm.at[0, :, pl.ds(pl.multiple_of(m * step, 128), step)], inverse_v.at[m], inv_sem.at[m]
        )

    def rhs_load(m):
        return pltpu.make_async_copy(
            rhs_hbm.at[0, pl.ds(pl.multiple_of(m * step, 8), step), :], rhs_v.at[m], rhs_sem.at[m]
        )

    others = [
        pltpu.make_async_copy(coupling_hbm.at[0], coupling_v, load_sem.at[0]),
        pltpu.make_async_copy(root_inverse_hbm, root_inverse_v, load_sem.at[1]),
        pltpu.make_async_copy(root_rhs_hbm, root_rhs_v, load_sem.at[2]),
        pltpu.make_async_copy(root_lower_hbm, root_lower_v, load_sem.at[3]),
    ]
    for m in range(chunks):
        inv_load(m).start()
        rhs_load(m).start()
    for copy in others:
        copy.start()

    barrier = pltpu.get_barrier_semaphore()
    pl.semaphore_signal(barrier, inc=1, device_id=at_row(1 - r), device_id_type=MESH)
    for o in range(1, cols):
        pl.semaphore_signal(barrier, inc=1, device_id=at_col(turn(c, o, cols)), device_id_type=MESH)

    @pl.loop(1, leaves)
    def _(o):
        pl.semaphore_signal(barrier, inc=1, device_id=at_leaf(turn(l, o, leaves)), device_id_type=MESH)

    solved[...] = jnp.zeros_like(solved)

    @pl.loop(0, chunks)
    def _(m):
        inv_load(m).wait()
        rhs_load(m).wait()
        solved[...] += mul(split(inverse_v[m]), split(rhs_v[m]))

    turned[...] = solved[...].T
    hi, lo = split(turned[...])
    turned_hi[...] = hi
    turned_lo[...] = lo
    others[0].wait()
    for k in range(seps):
        hi, lo = split(coupling_v[k] * coupled_ref[0, k].astype(F32))
        coup_hi[k] = hi
        coup_lo[k] = lo

    def make_term(half):
        at = pl.ds(pl.multiple_of(half * (nrhs // 2), 128), nrhs // 2)
        left = (turned_hi[at, :], turned_lo[at, :])

        @pl.loop(0, seps)
        def _(k):
            value = mul(left, (coup_hi[k], coup_lo[k]), NT)
            term[half, :, :, k] = value.reshape(cols, groups, 8, width)

    make_term(1 - r)
    pl.semaphore_wait(barrier, cols + leaves - 1)
    pair_copy = remote(term.at[1 - r], pair_in, pair_sem, 0, at_row(1 - r))
    pair_copy.start()
    make_term(r)
    pair_copy.wait()

    cols_copies = []
    for o in range(1, cols):
        to = turn(c, o, cols)
        pair_sum[to] = term[r, to] + pair_in[to]
        copy = remote(pair_sum.at[to], cols_in.at[o - 1], cols_sem, o - 1, at_col(to))
        copy.start()
        cols_copies.append(copy)
    pair_sum[c] = term[r, c] + pair_in[c]

    others[1].wait()
    others[3].wait()
    for k in range(seps):
        at = pl.ds(k * width, width)
        inv_k = root_inverse_v[k]
        if k:
            low = jnp.concatenate([root_lower_v[k, j] for j in range(k)], axis=1)
            known = (t_hi[0:k * width, 0:k * width], t_lo[0:k * width, 0:k * width])
            row = -mul(split(inv_k), split(mul(split(low), known)))
            hi, lo = split(row)
            t_hi[at, 0:k * width] = hi
            t_lo[at, 0:k * width] = lo
        hi, lo = split(inv_k)
        t_hi[at, at] = hi
        t_lo[at, at] = lo
        if k + 1 < seps:
            rest = pl.ds((k + 1) * width, (seps - 1 - k) * width)
            t_hi[at, rest] = jnp.zeros((width, (seps - 1 - k) * width), BF16)
            t_lo[at, rest] = jnp.zeros((width, (seps - 1 - k) * width), BF16)

    total = pair_sum[c]
    for o in range(1, cols):
        cols_copies[o - 1].wait()
        total = total + cols_in[o - 1]
    slab[...] = total.reshape(groups * seps, 8, width)

    def piece(x):
        return pl.ds(x * per, per)

    def leaf_copy(o):
        to = turn(l, o, leaves)
        return remote(slab.at[piece(to)], slab_in.at[o - 1], leaf_sem, o - 1, at_leaf(to))

    def back_copy(o):
        to = turn(l, o, leaves)
        return remote(mine, gathered.at[piece(l)], back_sem, o - 1, at_leaf(to))

    @pl.loop(1, leaves)
    def _(o):
        leaf_copy(o).start()

    mine[...] = slab[piece(l)]

    @pl.loop(0, chunks)
    def _(m):
        hi, lo = split(inverse_v[m].T)
        inv_hi[m] = hi
        inv_lo[m] = lo

    @pl.loop(1, leaves)
    def _(o):
        leaf_copy(o).wait()
        mine[...] += slab_in[o - 1]

    @pl.loop(1, leaves)
    def _(o):
        back_copy(o).start()

    gathered[piece(l)] = mine[...]
    others[2].wait()
    base = jnp.concatenate([root_rhs_v[k].T for k in range(seps)], axis=1)

    @pl.loop(1, leaves)
    def _(o):
        back_copy(o).wait()

    update = jnp.concatenate(
        [gathered[...].reshape(groups, seps, 8, width)[:, k].reshape(narrow, width) for k in range(seps)], axis=1
    )
    pending = base - update
    block = 2 * width
    blocks = seps // 2
    hi, lo = split(pending)
    forward = []
    for b in range(blocks):
        at = pl.ds(b * block, block)
        upto = (b + 1) * block
        forward.append(
            mul((hi[:, :upto], lo[:, :upto]), (t_hi[at, 0:upto], t_lo[at, 0:upto]), NT)
        )
    hi, lo = split(jnp.concatenate(forward, axis=1))
    solution_parts = []
    for b in range(blocks):
        at = pl.ds(b * block, block)
        rest = pl.ds(b * block, (blocks - b) * block)
        solution_parts.append(
            mul((hi[:, b * block:], lo[:, b * block:]), (t_hi[rest, at], t_lo[rest, at]), NN)
        )
    for k in range(seps):
        part_k = solution_parts[k // 2][:, (k % 2) * width:(k % 2 + 1) * width]
        root_all[r, c, :, k] = part_k.reshape(groups, 8, width)

    root_copies = []
    for o in range(1, cols):
        to = turn(c, o, cols)
        copy = remote(root_all.at[r, c], root_all.at[r, c], root_sem, o - 1, at_col(to))
        copy.start()
        root_copies.append(copy)

    def root_pair(i, which):
        return remote(root_all.at[r, which], root_all.at[r, which], root_pair_sem, i, at_row(1 - r))

    pair_copies = [root_pair(0, c)]
    pair_copies[0].start()
    for k in range(seps):
        part_k = solution_parts[k // 2][:, (k % 2) * width:(k % 2 + 1) * width]
        root_out[k] = part_k.T
    for o in range(1, cols):
        root_copies[o - 1].wait()
        copy = root_pair(o, turn(c, cols - o, cols))
        copy.start()
        pair_copies.append(copy)

    def make_resid(half):
        at = pl.ds(pl.multiple_of(half * (nrhs // 2), 128), nrhs // 2)
        value = root_all[half]
        left = split(jnp.concatenate([value[:, :, k].reshape(nrhs // 2, width) for k in range(seps)], axis=1))
        right = (coup_hi[...].reshape(seps * width, rows), coup_lo[...].reshape(seps * width, rows))
        return turned[at, :] - mul(left, right)

    turned[pl.ds(pl.multiple_of(r * (nrhs // 2), 128), nrhs // 2), :] = make_resid(r)
    for copy in pair_copies:
        copy.wait()
    other = 1 - r
    turned[pl.ds(pl.multiple_of(other * (nrhs // 2), 128), nrhs // 2), :] = make_resid(other)
    hi, lo = split(turned[...].T)
    resid_hi[...] = hi
    resid_lo[...] = lo

    def make_part(b):
        part[b] = mul((inv_hi[b], inv_lo[b]), (resid_hi[...], resid_lo[...]))

    def fin_pair(o):
        to = turn(c, o, cols)
        return remote(part.at[to], part_in.at[to], fin_pair_sem, o, at_row(0))

    def fin(o):
        to = turn(c, o, cols)
        return remote(part.at[r * cols + to], part_cols.at[o - 1], fin_sem, o - 1, at_col(to))

    @pl.when(r == 1)
    def _():
        for i in range(cols):
            o = (i + 1) % cols
            make_part(turn(c, o, cols))
            fin_pair(o).start()
        for i in range(cols):
            o = (i + 1) % cols
            to = turn(c, o, cols)

            @pl.when(to <= c)
            def _():
                make_part(cols + to)
                if o:
                    fin(o).start()
        for o in range(cols):
            fin_pair(o).wait_send()
        for o in range(1, cols):
            to = turn(c, o, cols)

            @pl.when(to < c)
            def _():
                fin(o).wait_send()

        leaf_out[0] = part[cols + c]
        for o in range(1, cols):
            source = turn(c, cols - o, cols)

            @pl.when(source > c)
            def _():
                fin(o).wait_recv()
                leaf_out[0] += part_cols[o - 1]

    @pl.when(r == 0)
    def _():
        for b in range(cols):
            make_part(b)
        for i in range(cols):
            o = (i + 1) % cols
            to = turn(c, o, cols)
            fin_pair_in = pltpu.make_async_remote_copy(
                src_ref=part.at[to], dst_ref=part_in.at[to],
                send_sem=fin_pair_sem.at[0, o], recv_sem=fin_pair_sem.at[1, o],
                device_id=at_row(1), device_id_type=MESH,
            )
            fin_pair_in.wait_recv()
            part[to] += part_in[to]
            if o:
                fin(o).start()
        leaf_out[0] = part[c]
        for o in range(1, cols):
            fin(o).wait_send()
            fin(o).wait_recv()
            leaf_out[0] += part_cols[o - 1]


def per_device(sizes, leaf_rhs, root_rhs, leaf_inverse, coupling, coupled, root_inverse, root_lower):
    leaves, cols, seps, width, order, rows, nrhs = sizes
    narrow = nrhs // (2 * cols)
    groups = narrow // 8
    per = groups * seps // leaves
    chunks = order // rows
    slab_shape = (groups, seps, 8, width)
    any_space = pl.BlockSpec(memory_space=pl.ANY)
    vmem = pl.BlockSpec(memory_space=pltpu.VMEM)
    smem = pl.BlockSpec(memory_space=pltpu.SMEM)
    total = seps * width
    V = pltpu.VMEM
    sem = lambda *shape: pltpu.SemaphoreType.DMA(shape)
    scratch = [
        V((chunks, rows, nrhs), F32), V((chunks, rows, rows), F32), V((seps, width, rows), F32),
        V((seps, width, narrow), F32), V((seps, width, width), F32), V((seps, seps, width, width), F32),
        V((rows, nrhs), F32), V((nrhs, rows), F32), V((nrhs, rows), BF16), V((nrhs, rows), BF16),
        V((seps, width, rows), BF16), V((seps, width, rows), BF16),
        V((chunks, rows, rows), BF16), V((chunks, rows, rows), BF16),
        V((8, width), F32), V((total, total), BF16), V((total, total), BF16),
        V((2, cols) + slab_shape, F32), V((cols,) + slab_shape, F32), V((cols,) + slab_shape, F32),
        V((cols - 1,) + slab_shape, F32), V((groups * seps, 8, width), F32),
        V((leaves - 1, per, 8, width), F32), V((per, 8, width), F32), V((groups * seps, 8, width), F32),
        V((2, cols) + slab_shape, F32), V((rows, nrhs), BF16), V((rows, nrhs), BF16),
        V((2 * cols, rows, nrhs), F32), V((cols, rows, nrhs), F32), V((cols - 1, rows, nrhs), F32),
        sem(4), sem(chunks), sem(chunks),
        sem(2, 1), sem(2, cols - 1), sem(2, leaves - 1), sem(2, leaves - 1),
        sem(2, cols - 1), sem(2, cols), sem(2, cols), sem(2, cols - 1),
    ]
    return pl.pallas_call(
        functools.partial(kernel, sizes),
        out_shape=(
            jax.ShapeDtypeStruct((1, rows, nrhs), F32),
            jax.ShapeDtypeStruct((seps, width, narrow), F32),
        ),
        in_specs=[any_space, any_space, any_space, any_space, smem, any_space, any_space],
        out_specs=(vmem, vmem),
        scratch_shapes=scratch,
        compiler_params=pltpu.CompilerParams(
            collective_id=0, has_side_effects=True, vmem_limit_bytes=56 * 1024 * 1024
        ),
    )(leaf_rhs, root_rhs, leaf_inverse, coupling, coupled, root_inverse, root_lower)


def solution(mesh):
    in_specs = (
        P("leaf", None, None),
        P(None, None, ("row", "col")),
        P("leaf", ("row", "col"), None),
        P("leaf", None, None, ("row", "col")),
        P("leaf", None),
        P(),
        P(),
    )
    out_specs = (P("leaf", ("row", "col"), None), P(None, None, ("row", "col")))
    leaves, cols = mesh.shape["leaf"], mesh.shape["col"]

    def run(leaf_rhs, root_rhs, leaf_inverse, coupling, coupled, root_inverse, root_lower):
        seps, width, nrhs = root_rhs.shape
        order = leaf_rhs.shape[1]
        sizes = (leaves, cols, seps, width, order, order // (2 * cols), nrhs)
        mapped = jax.shard_map(
            functools.partial(per_device, sizes), mesh=mesh, in_specs=in_specs, out_specs=out_specs,
            check_vma=False,
        )
        return mapped(leaf_rhs, root_rhs, leaf_inverse, coupling, coupled, root_inverse, root_lower)

    return run
```

time: 299 us -> 60.3 us (0.20); the launches traced: 296 us -> 60.1 us
  waiting for transfers between devices: 196 us -> 0 us
  matrix products: 78.6 us -> 0 us
  Pallas kernels: 0 us -> 54 us
  between operations: 15.2 us -> 0.64 us
    psum x1 -> x0, waiting for transfers between devices: 133 us -> none  [per_device(): total = lax.psum(term, ('leaf', 'row', 'col'))]
    dot_general x76 -> x0, matrix products: 78.6 us -> none  [the longest x28 29.1 us: per_device(): jnp.dot(root_lower[step, earlier], forward_parts[earlier], precision=high)]
    pallas_call x0 -> x1, Pallas kernels: none -> 54 us  [per_device(): pl.pallas_call(functools.partial(kernel, sizes), out_shape=(jax.ShapeDtyp...]
    reduce_scatter x1 -> x0, waiting for transfers between devices: 41.4 us -> none  [per_device(): lax.psum_scatter(lax.dot_general(inverse_rows, residual, (((0,), (0,)), (...]
    all_gather x1 -> x0, waiting for transfers between devices: 22.4 us -> none  [per_device(): full_root = lax.all_gather(root_mine, ('row', 'col'), axis=2, tiled=True)]
  transfers between devices with their start and end apart: 3 -> 0, of which waited for: 3 -> 0; matrix products, arithmetic and copies ran while one was open for 0% -> 0% of each run, Pallas kernels for 0% -> 0%
where the time goes in v1:
time: 60.3 us; the launch traced here: 60.1 us
  Pallas kernels  54 us (90%)
  local copies, waits for them, and re-layouts  5.44 us (9%)
  between operations  0.64 us (1%)
    pallas_call x1, Pallas kernels, per_device(): pl.pallas_call(functools.partial(kernel, sizes), out_shape=(jax.ShapeDtyp...  54 us
    unnamed x2, local copies, waits for them, and re-layouts  3.56 us
    pallas_call x1, local copies, waits for them, and re-layouts, per_device(): pl.pallas_call(functools.partial(kernel, sizes), out_shape=(jax.ShapeDtyp...  1.87 us

profile of v1, /device:TPU:0, one launch (start us, length us, event | category | flops | bytes accessed | tf_op | source)
XLA Modules:
  0.0 60.1 jit_solution(204477434861041312)
XLA Ops:
  0.6 1.9 %copy.9.root_rhs_hbm = f32[8,128,32]{2,1,0:T(8,128)} copy(f32[8,128,32]{1,2,0:T(8,128)} %param.8) | data formatting | bytes 262144 | tf_op args[1]
  2.5 54.0 %shard_map.86 = (f32[1,256,256]{2,1,0:T(8,128)}, f32[8,128,32]{2,1,0:T(8,128)}) custom-call(f32[1,2048,256]{2,1,0:T(8,128)} %rhs_hbm.1, f32[8,128,32]{2,1,0:T(8,128)} %copy.9.root_rhs_hbm, f32[1,256,2048]{2,1,0:T(8,128)} %inverse_hbm.1, f32[1,8,128,256]{3,2,1,0:T(8,128)} %coupling_hbm.1, s32[1,8]{1,0:T(1,128)} %coupled_ref.1, ...), custom_call_target="tpu_custom_call" | custom-call | tf_op jit(solution)/shard_map/pallas_call | solution.py:366
  56.5 1.9 %copy.10 = f32[8,128,32]{1,2,0:T(8,128)} copy(f32[8,128,32]{2,1,0:T(8,128)} %get-tuple-element.3) | data formatting | bytes 262144 | tf_op jit(solution)/shard_map/pallas_call | solution.py:366
  58.4 1.7 %copy.12 = f32[1,256,256]{2,1,0:T(8,128)} copy(f32[1,256,256]{2,1,0:T(8,128)} %get-tuple-element.6) | data formatting | bytes 524288

commit v2 on v1

--- a/solution.py
+++ b/solution.py
@@ -24,13 +24,17 @@
     return dot(a[0], b[0]) + (dot(a[0], b[1]) + dot(a[1], b[0]))
 
 
+def halves_of(groups, seps, leaves):
+    return 2 if (groups * seps // 2) % leaves == 0 else 1
+
+
 def kernel(
     sizes,
     rhs_hbm, root_rhs_hbm, inverse_hbm, coupling_hbm, coupled_ref, root_inverse_hbm, root_lower_hbm,
     leaf_out, root_out,
     rhs_v, inverse_v, coupling_v, root_rhs_v, root_inverse_v, root_lower_v,
     solved, turned, turned_hi, turned_lo, coup_hi, coup_lo, inv_hi, inv_lo,
-    t_full, t_hi, t_lo,
+    t_hi, t_lo,
     term, pair_in, pair_sum, cols_in, slab, slab_in, mine, gathered,
     root_all, resid_hi, resid_lo, part, part_in, part_cols,
     load_sem, rhs_sem, inv_sem,
@@ -39,7 +43,9 @@
     leaves, cols, seps, width, order, rows, nrhs = sizes
     narrow = nrhs // (2 * cols)
     groups = narrow // 8
-    per = groups * seps // leaves
+    halves = halves_of(groups, seps, leaves)
+    some = seps // halves
+    per = groups * some // leaves
     step = rows
     chunks = order // step
     l = lax.axis_index("leaf")
@@ -113,34 +119,41 @@
         coup_hi[k] = hi
         coup_lo[k] = lo
 
-    def make_term(half):
+    def make_term(half, h):
         at = pl.ds(pl.multiple_of(half * (nrhs // 2), 128), nrhs // 2)
         left = (turned_hi[at, :], turned_lo[at, :])
 
-        @pl.loop(0, seps)
+        @pl.loop(0, some)
         def _(k):
-            value = mul(left, (coup_hi[k], coup_lo[k]), NT)
-            term[half, :, :, k] = value.reshape(cols, groups, 8, width)
-
-    make_term(1 - r)
-    pl.semaphore_wait(barrier, cols + leaves - 1)
-    pair_copy = remote(term.at[1 - r], pair_in, pair_sem, 0, at_row(1 - r))
-    pair_copy.start()
-    make_term(r)
-    pair_copy.wait()
+            value = mul(left, (coup_hi[h * some + k], coup_lo[h * some + k]), NT)
+            term[half, h, :, :, k] = value.reshape(cols, groups, 8, width)
+
+    pair_starts = []
+    for h in range(halves):
+        make_term(1 - r, h)
+        if h == 0:
+            pl.semaphore_wait(barrier, cols + leaves - 1)
+        copy = remote(term.at[1 - r, h], pair_in.at[h], pair_sem, h, at_row(1 - r))
+        copy.start()
+        pair_starts.append(copy)
 
     cols_copies = []
-    for o in range(1, cols):
-        to = turn(c, o, cols)
-        pair_sum[to] = term[r, to] + pair_in[to]
-        copy = remote(pair_sum.at[to], cols_in.at[o - 1], cols_sem, o - 1, at_col(to))
-        copy.start()
-        cols_copies.append(copy)
-    pair_sum[c] = term[r, c] + pair_in[c]
+    for h in range(halves):
+        make_term(r, h)
+        pair_starts[h].wait()
+        for o in range(1, cols):
+            to = turn(c, o, cols)
+            pair_sum[h, to] = term[r, h, to] + pair_in[h, to]
+            i = h * (cols - 1) + o - 1
+            copy = remote(pair_sum.at[h, to], cols_in.at[i], cols_sem, i, at_col(to))
+            copy.start()
+            cols_copies.append(copy)
+        pair_sum[h, c] = term[r, h, c] + pair_in[h, c]
 
     others[1].wait()
     others[3].wait()
-    for k in range(seps):
+
+    def make_t(k):
         at = pl.ds(k * width, width)
         inv_k = root_inverse_v[k]
         if k:
@@ -158,55 +171,71 @@
             t_hi[at, rest] = jnp.zeros((width, (seps - 1 - k) * width), BF16)
             t_lo[at, rest] = jnp.zeros((width, (seps - 1 - k) * width), BF16)
 
-    total = pair_sum[c]
-    for o in range(1, cols):
-        cols_copies[o - 1].wait()
-        total = total + cols_in[o - 1]
-    slab[...] = total.reshape(groups * seps, 8, width)
-
     def piece(x):
         return pl.ds(x * per, per)
 
-    def leaf_copy(o):
+    def leaf_copy(h, o):
         to = turn(l, o, leaves)
-        return remote(slab.at[piece(to)], slab_in.at[o - 1], leaf_sem, o - 1, at_leaf(to))
-
-    def back_copy(o):
+        i = h * (leaves - 1) + o - 1
+        return remote(slab.at[h, piece(to)], slab_in.at[i], leaf_sem, i, at_leaf(to))
+
+    def back_copy(h, o):
         to = turn(l, o, leaves)
-        return remote(mine, gathered.at[piece(l)], back_sem, o - 1, at_leaf(to))
-
-    @pl.loop(1, leaves)
-    def _(o):
-        leaf_copy(o).start()
-
-    mine[...] = slab[piece(l)]
-
-    @pl.loop(0, chunks)
-    def _(m):
-        hi, lo = split(inverse_v[m].T)
-        inv_hi[m] = hi
-        inv_lo[m] = lo
-
-    @pl.loop(1, leaves)
-    def _(o):
-        leaf_copy(o).wait()
-        mine[...] += slab_in[o - 1]
-
-    @pl.loop(1, leaves)
-    def _(o):
-        back_copy(o).start()
-
-    gathered[piece(l)] = mine[...]
+        i = h * (leaves - 1) + o - 1
+        return remote(mine.at[h], gathered.at[h, piece(l)], back_sem, i, at_leaf(to))
+
+    done = 0
+    for h in range(halves):
+        upto = seps if h == halves - 1 else min(5, seps)
+        if h == halves - 1 and halves > 1:
+            upto = seps - 1
+        for k in range(done, upto):
+            make_t(k)
+        done = upto
+        total = pair_sum[h, c]
+        for o in range(1, cols):
+            cols_copies[h * (cols - 1) + o - 1].wait()
+            total = total + cols_in[h * (cols - 1) + o - 1]
+        slab[h] = total.reshape(groups * some, 8, width)
+
+        @pl.loop(1, leaves)
+        def _(o):
+            leaf_copy(h, o).start()
+
+        mine[h] = slab[h, piece(l)]
+
+    for k in range(done, seps):
+        make_t(k)
+
+    for h in range(halves):
+        @pl.loop(1, leaves)
+        def _(o):
+            leaf_copy(h, o).wait()
+            mine[h] += slab_in[h * (leaves - 1) + o - 1]
+
+        @pl.loop(1, leaves)
+        def _(o):
+            back_copy(h, o).start()
+
+        gathered[h, piece(l)] = mine[h]
+        if h == 0:
+            @pl.loop(0, chunks)
+            def _(m):
+                hi, lo = split(inverse_v[m].T)
+                inv_hi[m] = hi
+                inv_lo[m] = lo
+
     others[2].wait()
-    base = jnp.concatenate([root_rhs_v[k].T for k in range(seps)], axis=1)
-
-    @pl.loop(1, leaves)
-    def _(o):
-        back_copy(o).wait()
-
-    update = jnp.concatenate(
-        [gathered[...].reshape(groups, seps, 8, width)[:, k].reshape(narrow, width) for k in range(seps)], axis=1
-    )
+    base = jnp.concatenate([root_rhs_v[k] for k in range(seps)], axis=1)
+    updates = []
+    for h in range(halves):
+        @pl.loop(1, leaves)
+        def _(o):
+            back_copy(h, o).wait()
+
+        value = gathered[h].reshape(groups, some, 8, width)
+        updates += [value[:, k].reshape(narrow, width) for k in range(some)]
+    update = jnp.concatenate(updates, axis=1)
     pending = base - update
     block = 2 * width
     blocks = seps // 2
@@ -244,7 +273,7 @@
     pair_copies[0].start()
     for k in range(seps):
         part_k = solution_parts[k // 2][:, (k % 2) * width:(k % 2 + 1) * width]
-        root_out[k] = part_k.T
+        root_out[k] = part_k
     for o in range(1, cols):
         root_copies[o - 1].wait()
         copy = root_pair(o, turn(c, cols - o, cols))
@@ -338,9 +367,12 @@
     leaves, cols, seps, width, order, rows, nrhs = sizes
     narrow = nrhs // (2 * cols)
     groups = narrow // 8
-    per = groups * seps // leaves
+    halves = halves_of(groups, seps, leaves)
+    some = seps // halves
+    per = groups * some // leaves
     chunks = order // rows
     slab_shape = (groups, seps, 8, width)
+    half_shape = (groups, some, 8, width)
     any_space = pl.BlockSpec(memory_space=pl.ANY)
     vmem = pl.BlockSpec(memory_space=pltpu.VMEM)
     smem = pl.BlockSpec(memory_space=pltpu.SMEM)
@@ -349,25 +381,26 @@
     sem = lambda *shape: pltpu.SemaphoreType.DMA(shape)
     scratch = [
         V((chunks, rows, nrhs), F32), V((chunks, rows, rows), F32), V((seps, width, rows), F32),
-        V((seps, width, narrow), F32), V((seps, width, width), F32), V((seps, seps, width, width), F32),
+        V((seps, narrow, width), F32), V((seps, width, width), F32), V((seps, seps, width, width), F32),
         V((rows, nrhs), F32), V((nrhs, rows), F32), V((nrhs, rows), BF16), V((nrhs, rows), BF16),
         V((seps, width, rows), BF16), V((seps, width, rows), BF16),
         V((chunks, rows, rows), BF16), V((chunks, rows, rows), BF16),
-        V((8, width), F32), V((total, total), BF16), V((total, total), BF16),
-        V((2, cols) + slab_shape, F32), V((cols,) + slab_shape, F32), V((cols,) + slab_shape, F32),
-        V((cols - 1,) + slab_shape, F32), V((groups * seps, 8, width), F32),
-        V((leaves - 1, per, 8, width), F32), V((per, 8, width), F32), V((groups * seps, 8, width), F32),
+        V((total, total), BF16), V((total, total), BF16),
+        V((2, halves, cols) + half_shape, F32), V((halves, cols) + half_shape, F32),
+        V((halves, cols) + half_shape, F32), V((halves * (cols - 1),) + half_shape, F32),
+        V((halves, groups * some, 8, width), F32), V((halves * (leaves - 1), per, 8, width), F32),
+        V((halves, per, 8, width), F32), V((halves, groups * some, 8, width), F32),
         V((2, cols) + slab_shape, F32), V((rows, nrhs), BF16), V((rows, nrhs), BF16),
         V((2 * cols, rows, nrhs), F32), V((cols, rows, nrhs), F32), V((cols - 1, rows, nrhs), F32),
         sem(4), sem(chunks), sem(chunks),
-        sem(2, 1), sem(2, cols - 1), sem(2, leaves - 1), sem(2, leaves - 1),
+        sem(2, halves), sem(2, halves * (cols - 1)), sem(2, halves * (leaves - 1)), sem(2, halves * (leaves - 1)),
         sem(2, cols - 1), sem(2, cols), sem(2, cols), sem(2, cols - 1),
     ]
-    return pl.pallas_call(
+    leaf_result, root_result = pl.pallas_call(
         functools.partial(kernel, sizes),
         out_shape=(
             jax.ShapeDtypeStruct((1, rows, nrhs), F32),
-            jax.ShapeDtypeStruct((seps, width, narrow), F32),
+            jax.ShapeDtypeStruct((seps, narrow, width), F32),
         ),
         in_specs=[any_space, any_space, any_space, any_space, smem, any_space, any_space],
         out_specs=(vmem, vmem),
@@ -375,7 +408,8 @@
         compiler_params=pltpu.CompilerParams(
             collective_id=0, has_side_effects=True, vmem_limit_bytes=56 * 1024 * 1024
         ),
-    )(leaf_rhs, root_rhs, leaf_inverse, coupling, coupled, root_inverse, root_lower)
+    )(leaf_rhs, root_rhs.transpose(0, 2, 1), leaf_inverse, coupling, coupled, root_inverse, root_lower)
+    return leaf_result, root_result.transpose(0, 2, 1)
 
 
 def solution(mesh):

time: 60.3 us -> 55.7 us (0.924)
  Pallas kernels: 54 us -> 51.6 us
  local copies, waits for them, and re-layouts: 5.44 us -> 3.24 us
    pallas_call x1, Pallas kernels: 54 us -> 51.6 us  [per_device(): pl.pallas_call(functools.partial(kernel, sizes), out_shape=(jax.ShapeDtyp...]
    pallas_call x1 -> x0, local copies, waits for them, and re-layouts: 1.87 us -> none  [per_device(): pl.pallas_call(functools.partial(kernel, sizes), out_shape=(jax.ShapeDtyp...]
where the time goes in v2:
time: 55.7 us; the launch traced here: 55.5 us
  Pallas kernels  51.6 us (93%)
  local copies, waits for them, and re-layouts  3.24 us (6%)
  between operations  0.64 us (1%)
    pallas_call x1, Pallas kernels, per_device(): pl.pallas_call(functools.partial(kernel, sizes), out_shape=(jax.ShapeDtyp...  51.6 us
    unnamed x2, local copies, waits for them, and re-layouts  3.24 us

profile of v2, /device:TPU:0, one launch (start us, length us, event | category | flops | bytes accessed | tf_op | source)
XLA Modules:
  0.0 55.5 jit_solution(3593302246633430558)
XLA Ops:
  0.6 51.6 %shard_map.86 = (f32[1,256,256]{2,1,0:T(8,128)}, f32[8,32,128]{2,1,0:T(8,128)}) custom-call(f32[1,2048,256]{2,1,0:T(8,128)} %rhs_hbm.1, f32[8,32,128]{2,1,0:T(8,128)} %bitcast.2, f32[1,256,2048]{2,1,0:T(8,128)} %inverse_hbm.1, f32[1,8,128,256]{3,2,1,0:T(8,128)} %coupling_hbm.1, s32[1,8]{1,0:T(1,128)} %coupled_ref.1, f32[8,128,128]{2,1,0:T(8,128)} %root_inverse_hbm.1, ...), custom_call_target="tpu_custom_call" | custom-call | tf_op jit(solution)/shard_map/pallas_call | solution.py:399
  52.3 1.7 %copy.11 = f32[1,256,256]{2,1,0:T(8,128)} copy(f32[1,256,256]{2,1,0:T(8,128)} %get-tuple-element.8) | data formatting | bytes 524288
  53.9 1.6 %copy.12 = f32[8,128,32]{1,2,0:T(8,128)} copy(f32[8,128,32]{1,2,0:T(8,128)} %bitcast.3) | data formatting | bytes 262144

commit v3 on v2

--- a/solution.py
+++ b/solution.py
@@ -36,7 +36,7 @@
     solved, turned, turned_hi, turned_lo, coup_hi, coup_lo, inv_hi, inv_lo,
     t_hi, t_lo,
     term, pair_in, pair_sum, cols_in, slab, slab_in, mine, gathered,
-    root_all, resid_hi, resid_lo, part, part_in, part_cols,
+    root_all, resid_hi, resid_lo, part, part_in, relay_in, part_cols,
     load_sem, rhs_sem, inv_sem,
     pair_sem, cols_sem, leaf_sem, back_sem, root_sem, root_pair_sem, fin_pair_sem, fin_sem,
 ):
@@ -299,68 +299,120 @@
     def make_part(b):
         part[b] = mul((inv_hi[b], inv_lo[b]), (resid_hi[...], resid_lo[...]))
 
-    def fin_pair(o):
-        to = turn(c, o, cols)
-        return remote(part.at[to], part_in.at[to], fin_pair_sem, o, at_row(0))
-
-    def fin(o):
-        to = turn(c, o, cols)
-        return remote(part.at[r * cols + to], part_cols.at[o - 1], fin_sem, o - 1, at_col(to))
+    x = c + 1 - 2 * lax.rem(c, 2)
+    y = turn(c, 2, cols)
+    z = cols - 1 - c
+    upper, lower = pl.ds(0, rows // 2), pl.ds(rows // 2, rows // 2)
+
+    def fin_pair(t):
+        return remote(part.at[t], part_in.at[t], fin_pair_sem, t, at_row(1 - r))
+
+    def slot(t):
+        return r * cols + t
+
+    def ready(t):
+        @pl.when(r == 0)
+        def _():
+            fin_pair(t).wait_recv()
+            part[t] += part_in[t]
+
+        @pl.when(r == 1)
+        def _():
+            make_part(cols + t)
+
+    def if_any(nonzero):
+        return pl.when(jnp.logical_or(r == 0, nonzero))
+
+    sends = [
+        (remote(part.at[slot(z), upper], relay_in.at[0], fin_sem, 0, at_col(x)), z < c, y < x),
+        (remote(part.at[slot(z), lower], relay_in.at[1], fin_sem, 1, at_col(y)), z < c, x < y),
+        (remote(part.at[slot(x), upper], part_cols.at[0, upper], fin_sem, 2, at_col(x)), x < c, c < x),
+        (remote(part.at[slot(y), lower], part_cols.at[1, lower], fin_sem, 3, at_col(y)), y < c, c < y),
+        (
+            remote(part.at[slot(y), upper], part_cols.at[1, upper], fin_sem, 4, at_col(y)),
+            jnp.logical_or(y < c, y < x), jnp.logical_or(c < y, c < z),
+        ),
+        (
+            remote(part.at[slot(x), lower], part_cols.at[0, lower], fin_sem, 5, at_col(x)),
+            jnp.logical_or(x < c, x < y), jnp.logical_or(c < x, c < z),
+        ),
+    ]
+
+    def send(i):
+        @if_any(sends[i][1])
+        def _():
+            sends[i][0].start()
+
+    def receive(i, then):
+        @if_any(sends[i][2])
+        def _():
+            sends[i][0].wait_recv()
+            then()
+
+    for t in (z, x, y, c):
+        make_part(t)
+
+        @pl.when(r == 1)
+        def _():
+            fin_pair(t).start()
+
+    ready(z)
+    send(0)
+    send(1)
+    ready(x)
+    send(2)
+    ready(y)
+    send(3)
+
+    def add_upper():
+        part[slot(y), upper] += relay_in[0]
+
+    def add_lower():
+        part[slot(x), lower] += relay_in[1]
+
+    receive(0, add_upper)
+    send(4)
+    receive(1, add_lower)
+    send(5)
+    ready(c)
+    leaf_out[0] = part[slot(c)]
+
+    def add_part(way, at):
+        def add():
+            leaf_out[0, at] += part_cols[way, at]
+
+        return add
+
+    receive(2, add_part(0, upper))
+    receive(3, add_part(1, lower))
+    receive(4, add_part(1, upper))
+    receive(5, add_part(0, lower))
+    for copy, nonzero, _ in sends:
+        @if_any(nonzero)
+        def _():
+            copy.wait_send()
 
     @pl.when(r == 1)
     def _():
-        for i in range(cols):
-            o = (i + 1) % cols
-            make_part(turn(c, o, cols))
-            fin_pair(o).start()
-        for i in range(cols):
-            o = (i + 1) % cols
-            to = turn(c, o, cols)
-
-            @pl.when(to <= c)
-            def _():
-                make_part(cols + to)
-                if o:
-                    fin(o).start()
-        for o in range(cols):
-            fin_pair(o).wait_send()
-        for o in range(1, cols):
-            to = turn(c, o, cols)
-
-            @pl.when(to < c)
-            def _():
-                fin(o).wait_send()
-
-        leaf_out[0] = part[cols + c]
-        for o in range(1, cols):
-            source = turn(c, cols - o, cols)
-
-            @pl.when(source > c)
-            def _():
-                fin(o).wait_recv()
-                leaf_out[0] += part_cols[o - 1]
-
-    @pl.when(r == 0)
-    def _():
-        for b in range(cols):
-            make_part(b)
-        for i in range(cols):
-            o = (i + 1) % cols
-            to = turn(c, o, cols)
-            fin_pair_in = pltpu.make_async_remote_copy(
-                src_ref=part.at[to], dst_ref=part_in.at[to],
-                send_sem=fin_pair_sem.at[0, o], recv_sem=fin_pair_sem.at[1, o],
-                device_id=at_row(1), device_id_type=MESH,
-            )
-            fin_pair_in.wait_recv()
-            part[to] += part_in[to]
-            if o:
-                fin(o).start()
-        leaf_out[0] = part[c]
-        for o in range(1, cols):
-            fin(o).wait_send()
-            fin(o).wait_recv()
-            leaf_out[0] += part_cols[o - 1]
+        for t in range(cols):
+            fin_pair(t).wait_send()
+
+
+def hand_over(leaf_ref, root_ref, leaf_out, root_out, sems):
+    copies = []
+    pieces = sems.shape[0] // 2
+    deep = leaf_ref.shape[1] // pieces
+    for i in range(pieces):
+        at = pl.ds(i * deep, deep)
+        copies.append(pltpu.make_async_copy(leaf_ref.at[:, at], leaf_out.at[:, at], sems.at[i]))
+    deep = root_ref.shape[0] // pieces
+    for i in range(pieces):
+        at = pl.ds(i * deep, deep)
+        copies.append(pltpu.make_async_copy(root_ref.at[at], root_out.at[at], sems.at[pieces + i]))
+    for copy in copies:
+        copy.start()
+    for copy in copies:
+        copy.wait()
 
 
 def per_device(sizes, leaf_rhs, root_rhs, leaf_inverse, coupling, coupled, root_inverse, root_lower):
@@ -391,10 +443,11 @@
         V((halves, groups * some, 8, width), F32), V((halves * (leaves - 1), per, 8, width), F32),
         V((halves, per, 8, width), F32), V((halves, groups * some, 8, width), F32),
         V((2, cols) + slab_shape, F32), V((rows, nrhs), BF16), V((rows, nrhs), BF16),
-        V((2 * cols, rows, nrhs), F32), V((cols, rows, nrhs), F32), V((cols - 1, rows, nrhs), F32),
+        V((2 * cols, rows, nrhs), F32), V((cols, rows, nrhs), F32), V((2, rows // 2, nrhs), F32),
+        V((2, rows, nrhs), F32),
         sem(4), sem(chunks), sem(chunks),
         sem(2, halves), sem(2, halves * (cols - 1)), sem(2, halves * (leaves - 1)), sem(2, halves * (leaves - 1)),
-        sem(2, cols - 1), sem(2, cols), sem(2, cols), sem(2, cols - 1),
+        sem(2, cols - 1), sem(2, cols), sem(2, cols), sem(2, 6),
     ]
     leaf_result, root_result = pl.pallas_call(
         functools.partial(kernel, sizes),
@@ -409,6 +462,17 @@
             collective_id=0, has_side_effects=True, vmem_limit_bytes=56 * 1024 * 1024
         ),
     )(leaf_rhs, root_rhs.transpose(0, 2, 1), leaf_inverse, coupling, coupled, root_inverse, root_lower)
+    leaf_result, root_result = pl.pallas_call(
+        hand_over,
+        out_shape=(
+            jax.ShapeDtypeStruct(leaf_result.shape, F32),
+            jax.ShapeDtypeStruct(root_result.shape, F32),
+        ),
+        in_specs=[any_space, any_space],
+        out_specs=(any_space, any_space),
+        scratch_shapes=[sem(8)],
+        compiler_params=pltpu.CompilerParams(vmem_limit_bytes=60 * 1024 * 1024),
+    )(leaf_result, root_result)
     return leaf_result, root_result.transpose(0, 2, 1)
 
 

time: 55.7 us -> 62.7 us (1.13)
  Pallas kernels: 51.6 us -> 61.9 us
  local copies, waits for them, and re-layouts: 3.24 us -> 0 us
    pallas_call x0 -> x1, Pallas kernels: none -> 13.1 us  [per_device(): pl.pallas_call(hand_over, out_shape=(jax.ShapeDtypeStruct(leaf_result.sha...]
    unnamed x2 -> x0, local copies, waits for them, and re-layouts: 3.24 us -> none
    pallas_call x1, Pallas kernels: 51.6 us -> 48.8 us  [per_device(): pl.pallas_call(functools.partial(kernel, sizes), out_shape=(jax.ShapeDtyp...]
where the time goes in v3:
time: 62.7 us; the launch traced here: 62.5 us
  Pallas kernels  61.9 us (99%)
  between operations  0.64 us (1%)
    pallas_call x1, Pallas kernels, per_device(): pl.pallas_call(functools.partial(kernel, sizes), out_shape=(jax.ShapeDtyp...  48.8 us
    pallas_call x1, Pallas kernels, per_device(): pl.pallas_call(hand_over, out_shape=(jax.ShapeDtypeStruct(leaf_result.sha...  13.1 us

profile of v3, /device:TPU:0, one launch (start us, length us, event | category | flops | bytes accessed | tf_op | source)
XLA Modules:
  0.0 62.5 jit_solution(13950606896986196681)
XLA Ops:
  0.6 48.8 %shard_map.86 = (f32[1,256,256]{2,1,0:T(8,128)}, f32[8,32,128]{2,1,0:T(8,128)}) custom-call(f32[1,2048,256]{2,1,0:T(8,128)} %rhs_hbm.1, f32[8,32,128]{2,1,0:T(8,128)} %bitcast.2, f32[1,256,2048]{2,1,0:T(8,128)} %inverse_hbm.1, f32[1,8,128,256]{3,2,1,0:T(8,128)} %coupling_hbm.1, s32[1,8]{1,0:T(1,128)} %coupled_ref.1, f32[8,128,128]{2,1,0:T(8,128)} %root_inverse_hbm.1, ...), custom_call_target="tpu_custom_call" | custom-call | tf_op jit(solution)/shard_map/pallas_call | solution.py:452
  49.5 13.1 %shard_map.87 = (f32[1,256,256]{2,1,0:T(8,128)}, f32[8,32,128]{2,1,0:T(8,128)}) custom-call(f32[1,256,256]{2,1,0:T(8,128)} %get-tuple-element.6.leaf_ref, f32[8,32,128]{2,1,0:T(8,128)} %get-tuple-element.7.root_ref), custom_call_target="tpu_custom_call" | custom-call | tf_op jit(solution)/shard_map/pallas_call | solution.py:465

commit v4 on v3

--- a/solution.py
+++ b/solution.py
@@ -35,7 +35,7 @@
     rhs_v, inverse_v, coupling_v, root_rhs_v, root_inverse_v, root_lower_v,
     solved, turned, turned_hi, turned_lo, coup_hi, coup_lo, inv_hi, inv_lo,
     t_hi, t_lo,
-    term, pair_in, pair_sum, cols_in, slab, slab_in, mine, gathered,
+    term, pair_in, pair_sum, cols_relay, cols_in, slab, slab_in, mine, gathered,
     root_all, resid_hi, resid_lo, part, part_in, relay_in, part_cols,
     load_sem, rhs_sem, inv_sem,
     pair_sem, cols_sem, leaf_sem, back_sem, root_sem, root_pair_sem, fin_pair_sem, fin_sem,
@@ -55,6 +55,11 @@
     def turn(value, by, count):
         return lax.rem(value + by, count)
 
+    x = c + 1 - 2 * lax.rem(c, 2)
+    y = turn(c, 2, cols)
+    z = cols - 1 - c
+    first, second = pl.ds(0, groups // 2), pl.ds(groups // 2, groups // 2)
+
     def at_row(x):
         return {"leaf": l, "row": x, "col": c}
 
@@ -137,18 +142,35 @@
         copy.start()
         pair_starts.append(copy)
 
-    cols_copies = []
+    def cols_sends(h):
+        def one(i, src, dst, to):
+            return remote(src, dst, cols_sem, h * 6 + i, at_col(to))
+
+        return [
+            one(0, pair_sum.at[h, z, first], cols_relay.at[h, 0], x),
+            one(1, pair_sum.at[h, z, second], cols_relay.at[h, 1], y),
+            one(2, pair_sum.at[h, x, first], cols_in.at[h, 0, first], x),
+            one(3, pair_sum.at[h, y, second], cols_in.at[h, 1, second], y),
+            one(4, pair_sum.at[h, y, first], cols_in.at[h, 1, first], y),
+            one(5, pair_sum.at[h, x, second], cols_in.at[h, 0, second], x),
+        ]
+
+    cols_copies = [cols_sends(h) for h in range(halves)]
     for h in range(halves):
         make_term(r, h)
         pair_starts[h].wait()
-        for o in range(1, cols):
-            to = turn(c, o, cols)
+        for to in (z, x, y, c):
             pair_sum[h, to] = term[r, h, to] + pair_in[h, to]
-            i = h * (cols - 1) + o - 1
-            copy = remote(pair_sum.at[h, to], cols_in.at[i], cols_sem, i, at_col(to))
-            copy.start()
-            cols_copies.append(copy)
-        pair_sum[h, c] = term[r, h, c] + pair_in[h, c]
+        for i in range(4):
+            cols_copies[h][i].start()
+
+    for h in range(halves):
+        cols_copies[h][0].wait_recv()
+        pair_sum[h, y, first] += cols_relay[h, 0]
+        cols_copies[h][4].start()
+        cols_copies[h][1].wait_recv()
+        pair_sum[h, x, second] += cols_relay[h, 1]
+        cols_copies[h][5].start()
 
     others[1].wait()
     others[3].wait()
@@ -192,10 +214,11 @@
         for k in range(done, upto):
             make_t(k)
         done = upto
-        total = pair_sum[h, c]
-        for o in range(1, cols):
-            cols_copies[h * (cols - 1) + o - 1].wait()
-            total = total + cols_in[h * (cols - 1) + o - 1]
+        for i in range(2, 6):
+            cols_copies[h][i].wait_recv()
+        for i in range(6):
+            cols_copies[h][i].wait_send()
+        total = pair_sum[h, c] + cols_in[h, 0] + cols_in[h, 1]
         slab[h] = total.reshape(groups * some, 8, width)
 
         @pl.loop(1, leaves)
@@ -259,26 +282,38 @@
         part_k = solution_parts[k // 2][:, (k % 2) * width:(k % 2 + 1) * width]
         root_all[r, c, :, k] = part_k.reshape(groups, 8, width)
 
-    root_copies = []
-    for o in range(1, cols):
-        to = turn(c, o, cols)
-        copy = remote(root_all.at[r, c], root_all.at[r, c], root_sem, o - 1, at_col(to))
-        copy.start()
-        root_copies.append(copy)
-
-    def root_pair(i, which):
-        return remote(root_all.at[r, which], root_all.at[r, which], root_pair_sem, i, at_row(1 - r))
-
-    pair_copies = [root_pair(0, c)]
+    def root_send(i, which, at, to):
+        return remote(root_all.at[r, which, at], root_all.at[r, which, at], root_sem, i, at_col(to))
+
+    root_copies = [
+        root_send(0, c, first, x), root_send(1, c, second, y),
+        root_send(2, c, second, x), root_send(3, c, first, y),
+        root_send(4, x, first, y), root_send(5, y, second, x),
+    ]
+    for i in range(4):
+        root_copies[i].start()
+
+    pair_copies = [
+        remote(root_all.at[r, which], root_all.at[r, which], root_pair_sem, i, at_row(1 - r))
+        for i, which in enumerate((c, x, y, z))
+    ]
     pair_copies[0].start()
+    root_copies[0].wait_recv()
+    root_copies[4].start()
+    root_copies[1].wait_recv()
+    root_copies[5].start()
     for k in range(seps):
         part_k = solution_parts[k // 2][:, (k % 2) * width:(k % 2 + 1) * width]
         root_out[k] = part_k
-    for o in range(1, cols):
-        root_copies[o - 1].wait()
-        copy = root_pair(o, turn(c, cols - o, cols))
-        copy.start()
-        pair_copies.append(copy)
+    root_copies[2].wait_recv()
+    pair_copies[1].start()
+    root_copies[3].wait_recv()
+    pair_copies[2].start()
+    root_copies[4].wait_recv()
+    root_copies[5].wait_recv()
+    pair_copies[3].start()
+    for copy in root_copies:
+        copy.wait_send()
 
     def make_resid(half):
         at = pl.ds(pl.multiple_of(half * (nrhs // 2), 128), nrhs // 2)
@@ -299,9 +334,6 @@
     def make_part(b):
         part[b] = mul((inv_hi[b], inv_lo[b]), (resid_hi[...], resid_lo[...]))
 
-    x = c + 1 - 2 * lax.rem(c, 2)
-    y = turn(c, 2, cols)
-    z = cols - 1 - c
     upper, lower = pl.ds(0, rows // 2), pl.ds(rows // 2, rows // 2)
 
     def fin_pair(t):
@@ -398,21 +430,9 @@
             fin_pair(t).wait_send()
 
 
-def hand_over(leaf_ref, root_ref, leaf_out, root_out, sems):
-    copies = []
-    pieces = sems.shape[0] // 2
-    deep = leaf_ref.shape[1] // pieces
-    for i in range(pieces):
-        at = pl.ds(i * deep, deep)
-        copies.append(pltpu.make_async_copy(leaf_ref.at[:, at], leaf_out.at[:, at], sems.at[i]))
-    deep = root_ref.shape[0] // pieces
-    for i in range(pieces):
-        at = pl.ds(i * deep, deep)
-        copies.append(pltpu.make_async_copy(root_ref.at[at], root_out.at[at], sems.at[pieces + i]))
-    for copy in copies:
-        copy.start()
-    for copy in copies:
-        copy.wait()
+def hand_over(leaf_ref, root_ref, leaf_out, root_out):
+    leaf_out[...] = leaf_ref[...]
+    root_out[...] = root_ref[...]
 
 
 def per_device(sizes, leaf_rhs, root_rhs, leaf_inverse, coupling, coupled, root_inverse, root_lower):
@@ -439,15 +459,16 @@
         V((chunks, rows, rows), BF16), V((chunks, rows, rows), BF16),
         V((total, total), BF16), V((total, total), BF16),
         V((2, halves, cols) + half_shape, F32), V((halves, cols) + half_shape, F32),
-        V((halves, cols) + half_shape, F32), V((halves * (cols - 1),) + half_shape, F32),
+        V((halves, cols) + half_shape, F32),
+        V((halves, 2, groups // 2, some, 8, width), F32), V((halves, 2) + half_shape, F32),
         V((halves, groups * some, 8, width), F32), V((halves * (leaves - 1), per, 8, width), F32),
         V((halves, per, 8, width), F32), V((halves, groups * some, 8, width), F32),
         V((2, cols) + slab_shape, F32), V((rows, nrhs), BF16), V((rows, nrhs), BF16),
         V((2 * cols, rows, nrhs), F32), V((cols, rows, nrhs), F32), V((2, rows // 2, nrhs), F32),
         V((2, rows, nrhs), F32),
         sem(4), sem(chunks), sem(chunks),
-        sem(2, halves), sem(2, halves * (cols - 1)), sem(2, halves * (leaves - 1)), sem(2, halves * (leaves - 1)),
-        sem(2, cols - 1), sem(2, cols), sem(2, cols), sem(2, 6),
+        sem(2, halves), sem(2, halves * 6), sem(2, halves * (leaves - 1)), sem(2, halves * (leaves - 1)),
+        sem(2, 6), sem(2, cols), sem(2, cols), sem(2, 6),
     ]
     leaf_result, root_result = pl.pallas_call(
         functools.partial(kernel, sizes),
@@ -468,9 +489,8 @@
             jax.ShapeDtypeStruct(leaf_result.shape, F32),
             jax.ShapeDtypeStruct(root_result.shape, F32),
         ),
-        in_specs=[any_space, any_space],
-        out_specs=(any_space, any_space),
-        scratch_shapes=[sem(8)],
+        in_specs=[vmem, vmem],
+        out_specs=(vmem, vmem),
         compiler_params=pltpu.CompilerParams(vmem_limit_bytes=60 * 1024 * 1024),
     )(leaf_result, root_result)
     return leaf_result, root_result.transpose(0, 2, 1)

time: 62.7 us -> 53.9 us (0.86)
  Pallas kernels: 61.9 us -> 53.1 us
    pallas_call x1, Pallas kernels: 13.1 us -> 1.74 us  [per_device(): pl.pallas_call(hand_over, out_shape=(jax.ShapeDtypeStruct(leaf_result.sha...]
    pallas_call x1, Pallas kernels: 48.8 us -> 51.4 us  [per_device(): pl.pallas_call(functools.partial(kernel, sizes), out_shape=(jax.ShapeDtyp...]
where the time goes in v4:
time: 53.9 us; the launch traced here: 53.8 us
  Pallas kernels  53.1 us (99%)
  between operations  0.64 us (1%)
    pallas_call x1, Pallas kernels, per_device(): pl.pallas_call(functools.partial(kernel, sizes), out_shape=(jax.ShapeDtyp...  51.4 us
    pallas_call x1, Pallas kernels, per_device(): pl.pallas_call(hand_over, out_shape=(jax.ShapeDtypeStruct(leaf_result.sha...  1.74 us

profile of v4, /device:TPU:0, one launch (start us, length us, event | category | flops | bytes accessed | tf_op | source)
XLA Modules:
  0.0 53.8 jit_solution(11360627556162474915)
XLA Ops:
  0.6 51.4 %shard_map.86 = (f32[1,256,256]{2,1,0:T(8,128)}, f32[8,32,128]{2,1,0:T(8,128)}) custom-call(f32[1,2048,256]{2,1,0:T(8,128)} %rhs_hbm.1, f32[8,32,128]{2,1,0:T(8,128)} %bitcast.2, f32[1,256,2048]{2,1,0:T(8,128)} %inverse_hbm.1, f32[1,8,128,256]{3,2,1,0:T(8,128)} %coupling_hbm.1, s32[1,8]{1,0:T(1,128)} %coupled_ref.1, f32[8,128,128]{2,1,0:T(8,128)} %root_inverse_hbm.1, ...), custom_call_target="tpu_custom_call" | custom-call | tf_op jit(solution)/shard_map/pallas_call | solution.py:473
  52.0 1.7 %shard_map.87 = (f32[1,256,256]{2,1,0:T(8,128)}, f32[8,32,128]{2,1,0:T(8,128)}) custom-call(f32[1,256,256]{2,1,0:T(8,128)} %get-tuple-element.6.leaf_ref, f32[8,32,128]{2,1,0:T(8,128)} %get-tuple-element.7.root_ref), custom_call_target="tpu_custom_call" | custom-call | tf_op jit(solution)/shard_map/pallas_call | solution.py:486

commit v5 on v3

--- a/solution.py
+++ b/solution.py
@@ -89,8 +89,7 @@
     for m in range(chunks):
         inv_load(m).start()
         rhs_load(m).start()
-    for copy in others:
-        copy.start()
+    others[0].start()
 
     barrier = pltpu.get_barrier_semaphore()
     pl.semaphore_signal(barrier, inc=1, device_id=at_row(1 - r), device_id_type=MESH)
@@ -109,6 +108,8 @@
         rhs_load(m).wait()
         solved[...] += mul(split(inverse_v[m]), split(rhs_v[m]))
 
+    for copy in others[1:]:
+        copy.start()
     turned[...] = solved[...].T
     hi, lo = split(turned[...])
     turned_hi[...] = hi
@@ -398,21 +399,9 @@
             fin_pair(t).wait_send()
 
 
-def hand_over(leaf_ref, root_ref, leaf_out, root_out, sems):
-    copies = []
-    pieces = sems.shape[0] // 2
-    deep = leaf_ref.shape[1] // pieces
-    for i in range(pieces):
-        at = pl.ds(i * deep, deep)
-        copies.append(pltpu.make_async_copy(leaf_ref.at[:, at], leaf_out.at[:, at], sems.at[i]))
-    deep = root_ref.shape[0] // pieces
-    for i in range(pieces):
-        at = pl.ds(i * deep, deep)
-        copies.append(pltpu.make_async_copy(root_ref.at[at], root_out.at[at], sems.at[pieces + i]))
-    for copy in copies:
-        copy.start()
-    for copy in copies:
-        copy.wait()
+def hand_over(leaf_ref, root_ref, leaf_out, root_out):
+    leaf_out[...] = leaf_ref[...]
+    root_out[...] = root_ref[...]
 
 
 def per_device(sizes, leaf_rhs, root_rhs, leaf_inverse, coupling, coupled, root_inverse, root_lower):
@@ -468,9 +457,8 @@
             jax.ShapeDtypeStruct(leaf_result.shape, F32),
             jax.ShapeDtypeStruct(root_result.shape, F32),
         ),
-        in_specs=[any_space, any_space],
-        out_specs=(any_space, any_space),
-        scratch_shapes=[sem(8)],
+        in_specs=[vmem, vmem],
+        out_specs=(vmem, vmem),
         compiler_params=pltpu.CompilerParams(vmem_limit_bytes=60 * 1024 * 1024),
     )(leaf_result, root_result)
     return leaf_result, root_result.transpose(0, 2, 1)

time: 62.7 us -> 51.4 us (0.82)
  Pallas kernels: 61.9 us -> 50.6 us
    pallas_call x1, Pallas kernels: 13.1 us -> 1.74 us  [per_device(): pl.pallas_call(hand_over, out_shape=(jax.ShapeDtypeStruct(leaf_result.sha...]
where the time goes in v5:
time: 51.4 us; the launch traced here: 51.2 us
  Pallas kernels  50.6 us (98%)
  between operations  0.64 us (1%)
    pallas_call x1, Pallas kernels, per_device(): pl.pallas_call(functools.partial(kernel, sizes), out_shape=(jax.ShapeDtyp...  48.8 us
    pallas_call x1, Pallas kernels, per_device(): pl.pallas_call(hand_over, out_shape=(jax.ShapeDtypeStruct(leaf_result.sha...  1.74 us

profile of v5, /device:TPU:0, one launch (start us, length us, event | category | flops | bytes accessed | tf_op | source)
XLA Modules:
  0.0 51.2 jit_solution(3440040361482188357)
XLA Ops:
  0.6 48.8 %shard_map.86 = (f32[1,256,256]{2,1,0:T(8,128)}, f32[8,32,128]{2,1,0:T(8,128)}) custom-call(f32[1,2048,256]{2,1,0:T(8,128)} %rhs_hbm.1, f32[8,32,128]{2,1,0:T(8,128)} %bitcast.2, f32[1,256,2048]{2,1,0:T(8,128)} %inverse_hbm.1, f32[1,8,128,256]{3,2,1,0:T(8,128)} %coupling_hbm.1, s32[1,8]{1,0:T(1,128)} %coupled_ref.1, f32[8,128,128]{2,1,0:T(8,128)} %root_inverse_hbm.1, ...), custom_call_target="tpu_custom_call" | custom-call | tf_op jit(solution)/shard_map/pallas_call | solution.py:441
  49.5 1.7 %shard_map.87 = (f32[1,256,256]{2,1,0:T(8,128)}, f32[8,32,128]{2,1,0:T(8,128)}) custom-call(f32[1,256,256]{2,1,0:T(8,128)} %get-tuple-element.6.leaf_ref, f32[8,32,128]{2,1,0:T(8,128)} %get-tuple-element.7.root_ref), custom_call_target="tpu_custom_call" | custom-call | tf_op jit(solution)/shard_map/pallas_call | solution.py:454
